TPU v7x, 128 devices: a whole 4x4x4 slice. The times are simulated.
128 devices in a mesh: ctx: 32 (over x, z, y_hi), tp: 4 (over y_lo, core).
Axes of the slice: x: 4, y: 4 (y_hi: 2, y_lo: 2; y = y_hi * 2 + y_lo), z: 4, core: 2. Of those that a mesh axis runs over, the one named last changes fastest.
Arguments:
- queries: bfloat16 [8192, 4096], P('ctx', 'tp'), may hold values from -6 to 6
- keys: bfloat16 [8192, 512], P('ctx', 'tp'), may hold values from -5.5 to 5.5
- values: bfloat16 [8192, 512], P('ctx', 'tp'), may hold values from -6 to 6
- prior_keys: bfloat16 [8192, 512], P('ctx', 'tp'), may hold values from -6 to 6
- prior_values: bfloat16 [8192, 512], P('ctx', 'tp'), may hold values from -6 to 6
- out_weight: bfloat16 [4096, 8192], P(None, 'tp'), may hold values from -0.09375 to 0.09375
- ssm_x: bfloat16 [8192, 8192], P('ctx', 'tp'), may hold values from -6 to 6
- ssm_bc: bfloat16 [8192, 2, 1024], P('ctx', None, 'tp'), may hold values from -6 to 6
- gate_z: bfloat16 [8192, 8192], P('ctx', 'tp'), may hold values from -6 to 6
- conv_x: float32 [4, 8192], P(None, 'tp'), may hold values from -3 to 3
- conv_bc: float32 [4, 2, 1024], P(None, None, 'tp'), may hold values from -3 to 3
- conv_prior_x: bfloat16 [3, 8192], P(None, 'tp'), may hold values from -12 to 12
- conv_prior_bc: bfloat16 [3, 2, 1024], P(None, None, 'tp'), may hold values from -6 to 6
- step_dt: float32 [8192, 128], P('ctx', 'tp'), may hold values from 0.01 to 0.1
- log_decay: float32 [8192, 128], P('ctx', 'tp')
- skip_d: float32 [128], P('tp'), may hold values from 0.5 to 1.5
- ssm_prior: float32 [128, 64, 256], P('tp'), may hold values from -6 to 6
- norm_gain: float32 [8192], P('tp'), may hold values from 0.5 to 1.5
Outputs:
- attn_out: bfloat16 [8192, 8192], P('ctx', 'tp')
- ssm_out: bfloat16 [8192, 8192], P('ctx', 'tp')
All inputs are finite; a program needn't handle non-finite values.
Results may differ from a plain program's by a relative error of at most 0.017.
Values may be sent and summed in bfloat16 or wider, within the bound.
A program may use at most 320 MiB of HBM per device.

v0:
```python
import functools

import jax
import jax.numpy as jnp
from jax import lax
from jax.experimental import pallas as pl
from jax.experimental.pallas import tpu as pltpu
from jax.sharding import PartitionSpec as P

MESH = pl.DeviceIdType.MESH
F32 = jnp.float32
BF16 = jnp.bfloat16
HD = 128
CTX = 32
TP = 4
ROWS = 256
HEADS = 8
SH = 32
WIDE = 2048
PAIRS = 16
NSTATE = 256
MSG = 80
COEF = 1.4426950408889634 / (HD**0.5)
NT = (((1,), (1,)), ((), ()))
TN = (((0,), (0,)), ((), ()))


def dot(a, b, dims=(((1,), (0,)), ((), ()))):
    return lax.dot_general(a, b, dims, preferred_element_type=F32)


def exact_dot(a, b, dims):
    return lax.dot_general(
        a, b, dims, preferred_element_type=F32, precision=lax.Precision.HIGHEST
    )


def silu(v):
    return v / (1.0 + jnp.exp(-v))


def neighbour(c, dim, step):
    if dim == 0:
        return lax.rem(c + 8 * step + 32, 32)
    z = lax.rem(lax.div(c, 2), 4)
    return c + 2 * (lax.rem(z + step + 4, 4) - z)


def slot_of(c):
    return lax.div(c, 8) * 8 + lax.rem(c, 2) * 4 + lax.rem(lax.div(c, 2), 4)


def kernel(
    q_ref,
    k_ref,
    v_ref,
    pk_ref,
    pv_ref,
    w_hbm,
    x_ref,
    bc_ref,
    z_ref,
    taps_x,
    taps_bc,
    prior_x,
    prior_bc,
    dt_ref,
    ld_ref,
    skip_ref,
    prior_hbm,
    gain_ref,
    attn_ref,
    ssm_ref,
    kvb,
    acc,
    top,
    heads,
    w_ref,
    edge_x,
    edge_bc,
    ext,
    ext_bc,
    b_ref,
    c_ref,
    g_ref,
    aux,
    cum_t,
    xa,
    msg,
    got,
    state,
    back,
    incoming,
    squares,
    bar_unused,
    w_sem,
    prior_sem,
    y_send,
    y_recv,
    kv_send,
    kv_recv,
    edge_send,
    edge_recv,
    st_send,
    st_recv,
    in_send,
    in_recv,
    hd_send,
    hd_recv,
):
    c = lax.axis_index("ctx")
    t = lax.axis_index("tp")
    mate = c + 1 - 2 * lax.rem(c, 2)

    def remote(src, dst, send, recv, dev):
        return pltpu.make_async_remote_copy(
            src_ref=src,
            dst_ref=dst,
            send_sem=send,
            recv_sem=recv,
            device_id=dev,
            device_id_type=MESH,
        )

    w_copy = pltpu.make_async_copy(w_hbm, w_ref, w_sem)
    w_copy.start()
    prior_copy = pltpu.make_async_copy(
        prior_hbm.at[pl.ds(pl.multiple_of(c * 64, 64), 64)], state, prior_sem
    )
    prior_copy.start()
    own = slot_of(c)
    kvb[own, 0] = k_ref[...]
    kvb[own, 1] = v_ref[...]
    kvb[own, 2] = pk_ref[...]
    kvb[own, 3] = pv_ref[...]

    barrier = pltpu.get_barrier_semaphore()

    def greet_ctx(i, carry):
        pl.semaphore_signal(
            barrier, inc=1, device_id=(lax.rem(c + i, CTX), t), device_id_type=MESH
        )
        return carry

    def greet_tp(i, carry):
        pl.semaphore_signal(
            barrier, inc=1, device_id=(c, lax.rem(t + i, TP)), device_id_type=MESH
        )
        return carry

    lax.fori_loop(1, CTX, greet_ctx, 0)
    lax.fori_loop(1, TP, greet_tp, 0)
    pl.semaphore_wait(barrier, CTX - 1 + TP - 1)

    def first(half):
        return 0 if half == 0 else 1

    def piece(slot, half, quarter):
        if quarter is None:
            return kvb.at[slot, pl.ds(2 * half, 2)]
        return kvb.at[slot, 2 * half + quarter]

    def kv_copy(chunk, half, quarter, send, dest):
        slot = slot_of(chunk)
        ref = piece(slot, half, quarter)
        recv = kv_recv.at[slot, half, 0 if quarter is None else quarter]
        return remote(ref, ref, send, recv, (dest, t))

    def base(p):
        return c if p == 0 else mate

    def send_desc(kind, p, r, half, way):
        dim1, dim2 = first(half), 1 - first(half)
        step = 1 - 2 * way
        if kind == "p1a":
            return kv_copy(
                base(p), half, None, kv_send.at[p, 0, half, way], neighbour(c, dim1, step)
            )
        if kind == "p1b":
            chunk = neighbour(base(p), dim1, -step)
            return kv_copy(
                chunk, half, way, kv_send.at[p, 1, half, way], neighbour(c, dim1, step)
            )
        row = neighbour(base(p), dim1, r)
        if kind == "p2a":
            return kv_copy(
                row, half, None, kv_send.at[p, 2 + r, half, way], neighbour(c, dim2, step)
            )
        chunk = neighbour(row, dim2, -step)
        return kv_copy(
            chunk, half, way, kv_send.at[p, 6 + r, half, way], neighbour(c, dim2, step)
        )

    def wait_whole(chunk, half):
        kv_copy(chunk, half, None, kv_send.at[0, 0, 0, 0], c).wait_recv()

    def wait_split(chunk, half):
        for quarter in range(2):
            kv_copy(chunk, half, quarter, kv_send.at[0, 0, 0, 0], c).wait_recv()

    def each(fn):
        for half in range(2):
            for way in range(2):
                fn(half, way)

    def stage_a(p):
        each(lambda half, way: send_desc("p1a", p, 0, half, way).start())
        each(lambda half, way: send_desc("p2a", p, 0, half, way).start())

    def stage_b(p):
        def got_one(half, way):
            wait_whole(neighbour(base(p), first(half), 2 * way - 1), half)
            send_desc("p1b", p, 0, half, way).start()

        each(got_one)
        for r in (1, 3):
            each(lambda half, way: send_desc("p2a", p, r, half, way).start())

    def stage_c(p):
        for half in range(2):
            wait_split(neighbour(base(p), first(half), 2), half)
        each(lambda half, way: send_desc("p2a", p, 2, half, way).start())
        forward(p, 0)

    def forward(p, r):
        def got_one(half, way):
            row = neighbour(base(p), first(half), r)
            wait_whole(neighbour(row, 1 - first(half), 2 * way - 1), half)
            send_desc("p2b", p, r, half, way).start()

        each(got_one)

    def stage_d(p):
        forward(p, 1)
        forward(p, 3)

    def stage_e(p):
        forward(p, 2)

    def stage_f(p):
        def one(r, carry):
            for half in range(2):
                row = neighbour(base(p), first(half), r)
                wait_split(neighbour(row, 1 - first(half), 2), half)
            return carry

        lax.fori_loop(0, 4, one, 0)

    y_copy = remote(kvb.at[own], kvb.at[own], y_send, y_recv, (mate, t))
    y_got = remote(kvb.at[slot_of(mate)], kvb.at[slot_of(mate)], y_send, y_recv, (mate, t))

    following = lax.rem(c + 1, CTX)
    edge_copies = [
        remote(x_ref.at[pl.ds(ROWS - 16, 16)], edge_x, edge_send.at[0], edge_recv.at[0], (following, t)),
        remote(bc_ref.at[pl.ds(ROWS - 16, 16)], edge_bc, edge_send.at[1], edge_recv.at[1], (following, t)),
    ]
    for copy in edge_copies:
        copy.start()
    y_copy.start()
    stage_a(0)

    row_i = lax.broadcasted_iota(jnp.int32, (ROWS, ROWS), 0)
    col_i = lax.broadcasted_iota(jnp.int32, (ROWS, ROWS), 1)
    lower = row_i >= col_i
    ones_low = jnp.where(lower, 1.0, 0.0).astype(F32)
    ld = ld_ref[...]
    cum = exact_dot(ones_low, ld, (((1,), (0,)), ((), ())))
    cum_t[...] = exact_dot(ld, ones_low, (((0,), (1,)), ((), ())))
    dt = dt_ref[...]
    aux[:, 0:32] = cum
    aux[:, 32:64] = dt
    aux[:, 64:96] = jnp.exp(cum[ROWS - 1 : ROWS] - cum) * dt
    aux[:, 96:128] = jnp.exp(cum)

    for copy in edge_copies:
        copy.wait_recv()

    at_start = c == 0

    def conv(buffer, edge, own_prior, here, taps):
        before = jnp.where(at_start, own_prior.astype(F32), edge.astype(F32)[8:16])
        buffer[0:8, :] = before
        buffer[8 : 8 + ROWS, :] = here.astype(F32)
        total = taps[0:1] * buffer[5 : 5 + ROWS, :]
        for k in range(1, 4):
            total = total + taps[k : k + 1] * buffer[5 + k : 5 + k + ROWS, :]
        return silu(total)

    proj = conv(ext_bc, edge_bc[...], prior_bc[...], bc_ref[...], taps_bc[...])
    b_ref[...] = proj[:, :NSTATE].astype(BF16)
    c_ref[...] = proj[:, NSTATE:].astype(BF16)
    g_ref[...] = dot(c_ref[...], b_ref[...], NT)

    left_half = lax.broadcasted_iota(jnp.int32, (ROWS, 128), 1) < 64

    def columns(pair):
        return pl.ds(pl.multiple_of(pair * 128, 128), 128)

    def rolled(pair):
        return pltpu.roll(aux[...], 128 - 2 * pair, 1)

    def spread(lanes, at):
        return jnp.where(left_half, lanes[:, at : at + 1], lanes[:, at + 1 : at + 2])

    def state_copy(h):
        return remote(msg.at[h], got.at[c], st_send.at[h], st_recv.at[c], (h, t))

    def local_states(pair, carry):
        cols = columns(pair)
        act = conv(ext, edge_x[:, cols], prior_x[:, cols], x_ref[:, cols], taps_x[:, cols])
        xa[:, cols] = act
        lanes = rolled(pair)
        weighted = (act * spread(lanes, 64)).astype(BF16)
        made = dot(weighted, b_ref[...], TN).astype(BF16)
        row = lax.broadcasted_iota(jnp.int32, (16, NSTATE), 0)
        for sub in range(2):
            h = 2 * pair + sub
            msg[h, 0:64, :] = made[64 * sub : 64 * sub + 64]
            total = jnp.broadcast_to(lanes[ROWS - 1 : ROWS, sub : sub + 1], (16, NSTATE))
            hi = total.astype(BF16).astype(F32)
            mid = (total - hi).astype(BF16).astype(F32)
            low = total - hi - mid
            parts = jnp.where(row == 0, hi, jnp.where(row == 1, mid, jnp.where(row == 2, low, 0.0)))
            msg[h, 64:80, :] = parts.astype(BF16)

            @pl.when(h != c)
            def _():
                state_copy(h).start()

            @pl.when(h == c)
            def _():
                got[c] = msg[h]

        @pl.when(pair == 6)
        def _():
            stage_b(0)

        @pl.when(pair == 12)
        def _():
            y_got.wait_recv()
            stage_a(1)

        return carry

    lax.fori_loop(0, PAIRS, local_states, 0)
    stage_c(0)

    def within_block(pair, carry):
        cols = columns(pair)
        lanes = rolled(pair)
        act = xa[:, cols]
        scaled = (act * spread(lanes, 32)).astype(BF16)
        parts = []
        for sub in range(2):
            h = 2 * pair + sub
            diff = lanes[:, sub : sub + 1] - cum_t[pl.ds(h, 1), :]
            decay = jnp.exp(jnp.where(lower, diff, -1e30))
            parts.append(dot((g_ref[...] * decay).astype(BF16), scaled))
        xa[:, cols] = jnp.where(left_half, parts[0], parts[1]) + skip_ref[:, cols] * act

        @pl.when(pair == 6)
        def _():
            stage_b(1)

        @pl.when(pair == 12)
        def _():
            stage_d(0)

        return carry

    lax.fori_loop(0, PAIRS, within_block, 0)
    stage_e(0)

    acc[...] = jnp.zeros_like(acc)
    top[...] = jnp.full(top.shape, -1e30, F32)

    def attend(h, keys, vals, allowed):
        query = q_ref[:, pl.ds(pl.multiple_of(h * HD, HD), HD)]
        scores = dot(query, keys, NT)
        if allowed is not None:
            scores = jnp.where(allowed, scores, -1e30)
        return scores

    def absorb(h, scores, vals):
        before = top[h]
        new = jnp.maximum(before, jnp.max(scores, axis=1, keepdims=True))
        top[h] = new
        shrink = jnp.exp2((before - new) * COEF)
        weights = jnp.exp2((scores - new[:, 0:1]) * COEF).astype(BF16)
        wide = jnp.concatenate([vals, jnp.ones_like(vals)], axis=1)
        acc[h] = acc[h] * jnp.concatenate([shrink, shrink], axis=1) + dot(weights, wide)

    def cached(g, carry):
        @pl.when(g == 1)
        def _():
            stage_c(1)

        @pl.when(g == 3)
        def _():
            stage_d(1)
            stage_e(1)

        @pl.when(g == 4)
        def _():
            stage_f(0)

        @pl.when(g == 7)
        def _():
            stage_f(1)

        plane = jnp.where((g == 3) | (g >= 5), 1, 0)
        far = jnp.where(
            (g == 0) | (g == 3), 0, jnp.where((g == 1) | (g == 5), 1, jnp.where((g == 2) | (g == 6), 3, 2))
        )
        x_at = lax.rem(lax.div(c, 8) + far, 4)
        y_at = lax.rem(lax.rem(c, 2) + plane, 2)
        slot = x_at * 8 + y_at * 4
        keys = kvb[pl.ds(slot, 4), 2].reshape(4 * ROWS, HD)
        vals = kvb[pl.ds(slot, 4), 3].reshape(4 * ROWS, HD)

        def two(i, carry2):
            s0 = attend(2 * i, keys, vals, None)
            s1 = attend(2 * i + 1, keys, vals, None)
            absorb(2 * i, s0, vals)
            absorb(2 * i + 1, s1, vals)
            return carry2

        lax.fori_loop(0, HEADS // 2, two, 0)
        return carry

    lax.fori_loop(0, 8, cached, 0)

    prior_copy.wait()

    def back_copy(j):
        here = pl.ds(pl.multiple_of(c * 64, 64), 64)
        return remote(back.at[j], incoming.at[here], in_send.at[j], in_recv.at[c], (j, t))

    def scan(j, carry):
        @pl.when(j != c)
        def _():
            remote(msg.at[j], got.at[j], st_send.at[j], st_recv.at[j], (j, t)).wait_recv()

        now = state[...]
        back[j] = now.astype(BF16)

        @pl.when(j != c)
        def _():
            back_copy(j).start()

        @pl.when(j == c)
        def _():
            incoming[pl.ds(pl.multiple_of(c * 64, 64), 64), :] = now.astype(BF16)

        tail = got[j, 64:80, :].astype(F32)
        total = tail[0:1] + tail[1:2] + tail[2:3]
        state[...] = jnp.exp(total) * now + got[j, 0:64, :].astype(F32)
        return carry

    lax.fori_loop(0, CTX, scan, 0)

    def head_copy(h, i):
        cols = pl.ds(pl.multiple_of((t * HEADS + h) * HD, HD), HD)
        return remote(
            heads.at[:, cols],
            heads.at[:, cols],
            hd_send.at[h, i],
            hd_recv.at[t, h],
            (c, lax.rem(t + i, TP)),
        )

    def head_block(h, carry):
        def whole(g, carry2):
            slot = g * 4
            keys = kvb[pl.ds(slot, 4), 0].reshape(4 * ROWS, HD)
            vals = kvb[pl.ds(slot, 4), 1].reshape(4 * ROWS, HD)
            absorb(h, attend(h, keys, vals, None), vals)
            return carry2

        lax.fori_loop(0, 2 * lax.div(c, 8), whole, 0)

        def single(j, carry2):
            slot = slot_of(j)
            vals = kvb[slot, 1]
            absorb(h, attend(h, kvb[slot, 0], vals, None), vals)
            return carry2

        lax.fori_loop(lax.div(c, 8) * 8, c, single, 0)
        vals = kvb[own, 1]
        absorb(h, attend(h, kvb[own, 0], vals, lower), vals)
        full = acc[h]
        cols = pl.ds(pl.multiple_of((t * HEADS + h) * HD, HD), HD)
        heads[:, cols] = (full[:, :HD] / full[:, HD:]).astype(BF16)
        for i in range(1, TP):
            head_copy(h, i).start()
        return carry

    lax.fori_loop(0, HEADS, head_block, 0)

    def in_wait(j, carry):
        @pl.when(j != c)
        def _():
            rows = pl.ds(pl.multiple_of(j * 64, 64), 64)
            remote(back.at[j], incoming.at[rows], in_send.at[j], in_recv.at[j], (j, t)).wait_recv()

        return carry

    lax.fori_loop(0, CTX, in_wait, 0)
    squares[...] = jnp.zeros_like(squares)

    def mix(pair, carry):
        cols = columns(pair)
        lanes = rolled(pair)
        earlier = dot(c_ref[...], incoming[cols, :], NT)
        mixed = xa[:, cols] + spread(lanes, 96) * earlier
        gated = mixed * silu(z_ref[:, cols].astype(F32))
        squares[...] += gated * gated
        xa[:, cols] = gated
        return carry

    lax.fori_loop(0, PAIRS, mix, 0)
    mean = jnp.sum(squares[...], axis=1, keepdims=True) * (1.0 / WIDE)
    squares[...] = jnp.broadcast_to(lax.rsqrt(mean + 1e-05), squares.shape)

    def norm(pair, carry):
        cols = columns(pair)
        ssm_ref[:, cols] = (xa[:, cols] * squares[...] * gain_ref[:, cols]).astype(BF16)
        return carry

    lax.fori_loop(0, PAIRS, norm, 0)

    def head_wait(h, carry):
        for i in range(1, TP):
            src = lax.rem(t + i, TP)
            cols = pl.ds(pl.multiple_of((src * HEADS + h) * HD, HD), HD)
            remote(
                heads.at[:, cols], heads.at[:, cols], hd_send.at[h, i], hd_recv.at[src, h], (c, src)
            ).wait_recv()
        return carry

    lax.fori_loop(0, HEADS, head_wait, 0)
    w_copy.wait()

    def project(n, carry):
        cols = pl.ds(pl.multiple_of(n * 256, 256), 256)
        attn_ref[:, cols] = dot(heads[...], w_ref[:, cols]).astype(BF16)
        return carry

    lax.fori_loop(0, WIDE // 256, project, 0)

    for copy in edge_copies:
        copy.wait_send()
    y_copy.wait_send()
    for p in range(2):
        each(lambda half, way: send_desc("p1a", p, 0, half, way).wait_send())
        each(lambda half, way: send_desc("p1b", p, 0, half, way).wait_send())

        def sent(r, carry):
            each(lambda half, way: send_desc("p2a", p, r, half, way).wait_send())
            each(lambda half, way: send_desc("p2b", p, r, half, way).wait_send())
            return carry

        lax.fori_loop(0, 4, sent, 0)

    def states_sent(j, carry):
        @pl.when(j != c)
        def _():
            state_copy(j).wait_send()
            back_copy(j).wait_send()

        return carry

    lax.fori_loop(0, CTX, states_sent, 0)

    def heads_sent(h, carry):
        for i in range(1, TP):
            head_copy(h, i).wait_send()
        return carry

    lax.fori_loop(0, HEADS, heads_sent, 0)


def per_device(
    queries,
    keys,
    values,
    prior_keys,
    prior_values,
    out_weight,
    ssm_x,
    ssm_bc,
    gate_z,
    conv_x,
    conv_bc,
    conv_prior_x,
    conv_prior_bc,
    step_dt,
    log_decay,
    skip_d,
    ssm_prior,
    norm_gain,
):
    vm = pl.BlockSpec(memory_space=pltpu.VMEM)
    anywhere = pl.BlockSpec(memory_space=pl.ANY)
    pad = ((5, 0), (0, 0))
    return pl.pallas_call(
        kernel,
        out_shape=(
            jax.ShapeDtypeStruct((ROWS, WIDE), BF16),
            jax.ShapeDtypeStruct((ROWS, WIDE), BF16),
        ),
        in_specs=[vm] * 5 + [anywhere] + [vm] * 10 + [anywhere, vm],
        out_specs=(vm, vm),
        scratch_shapes=[
            pltpu.VMEM((CTX, 4, ROWS, HD), BF16),
            pltpu.VMEM((HEADS, ROWS, 2 * HD), F32),
            pltpu.VMEM((HEADS, ROWS, HD), F32),
            pltpu.VMEM((ROWS, TP * HEADS * HD), BF16),
            pltpu.VMEM((TP * HEADS * HD, WIDE), BF16),
            pltpu.VMEM((16, WIDE), BF16),
            pltpu.VMEM((16, 2 * NSTATE), BF16),
            pltpu.VMEM((ROWS + 8, 128), F32),
            pltpu.VMEM((ROWS + 8, 2 * NSTATE), F32),
            pltpu.VMEM((ROWS, NSTATE), BF16),
            pltpu.VMEM((ROWS, NSTATE), BF16),
            pltpu.VMEM((ROWS, ROWS), F32),
            pltpu.VMEM((ROWS, 128), F32),
            pltpu.VMEM((SH, ROWS), F32),
            pltpu.VMEM((ROWS, WIDE), F32),
            pltpu.VMEM((SH, MSG, NSTATE), BF16),
            pltpu.VMEM((CTX, MSG, NSTATE), BF16),
            pltpu.VMEM((64, NSTATE), F32),
            pltpu.VMEM((CTX, 64, NSTATE), BF16),
            pltpu.VMEM((WIDE, NSTATE), BF16),
            pltpu.VMEM((ROWS, 128), F32),
            pltpu.VMEM((8, 128), F32),
            pltpu.SemaphoreType.DMA,
            pltpu.SemaphoreType.DMA,
            pltpu.SemaphoreType.DMA,
            pltpu.SemaphoreType.DMA,
            pltpu.SemaphoreType.DMA((2, 10, 2, 2)),
            pltpu.SemaphoreType.DMA((CTX, 2, 2)),
            pltpu.SemaphoreType.DMA((2,)),
            pltpu.SemaphoreType.DMA((2,)),
            pltpu.SemaphoreType.DMA((CTX,)),
            pltpu.SemaphoreType.DMA((CTX,)),
            pltpu.SemaphoreType.DMA((CTX,)),
            pltpu.SemaphoreType.DMA((CTX,)),
            pltpu.SemaphoreType.DMA((HEADS, TP)),
            pltpu.SemaphoreType.DMA((TP, HEADS)),
        ],
        compiler_params=pltpu.CompilerParams(
            collective_id=0, has_side_effects=True, vmem_limit_bytes=60 * 2**20
        ),
        name="hybrid",
    )(
        queries,
        keys,
        values,
        prior_keys,
        prior_values,
        out_weight,
        ssm_x,
        ssm_bc.reshape(ROWS, 2 * NSTATE),
        gate_z,
        conv_x,
        conv_bc.reshape(4, 2 * NSTATE),
        jnp.pad(conv_prior_x, pad),
        jnp.pad(conv_prior_bc.reshape(3, 2 * NSTATE), pad),
        step_dt,
        log_decay,
        jnp.repeat(skip_d, 64).reshape(1, WIDE),
        ssm_prior.reshape(WIDE, NSTATE),
        norm_gain.reshape(1, WIDE),
    )


def solution(mesh):
    in_specs = (
        P("ctx", "tp"),
        P("ctx", "tp"),
        P("ctx", "tp"),
        P("ctx", "tp"),
        P("ctx", "tp"),
        P(None, "tp"),
        P("ctx", "tp"),
        P("ctx", None, "tp"),
        P("ctx", "tp"),
        P(None, "tp"),
        P(None, None, "tp"),
        P(None, "tp"),
        P(None, None, "tp"),
        P("ctx", "tp"),
        P("ctx", "tp"),
        P("tp"),
        P("tp", None, None),
        P("tp"),
    )
    out_specs = (P("ctx", "tp"), P("ctx", "tp"))
    return jax.shard_map(
        per_device, mesh=mesh, in_specs=in_specs, out_specs=out_specs, check_vma=False
    )
```

profile of v0, /device:TPU:118, one launch (start us, length us, event | category | flops | bytes accessed | tf_op | source)
XLA Modules:
  0.0 202.1 jit_solution(7831480649622660768)
XLA Ops:
  0.6 0.7 copy.24
  1.3 0.6 pad.9.prior_bc
  1.9 1.3 copy.23
  3.2 0.7 broadcast_in_dim.3
  3.9 0.7 reshape_reshape.3.skip_ref
  4.6 1.3 pad.8.prior_x
  6.0 1.5 copy.20.dt_ref
  7.5 1.5 copy.21.ld_ref
  9.0 1.7 copy.22
  10.7 186.8 %hybrid.1 = (bf16[256,2048]{1,0:T(8,128)(2,1)}, bf16[256,2048]{1,0:T(8,128)(2,1)}) custom-call(bf16[256,1024]{1,0:T(8,128)(2,1)} %q_ref.1, bf16[256,128]{1,0:T(8,128)(2,1)} %k_ref.1, bf16[256,128]{1,0:T(8,128)(2,1)} %v_ref.1, bf16[256,128]{1,0:T(8,128)(2,1)} %pk_ref.1, bf16[256,128]{1,0:T(8,128)(2,1)} %pv_ref.1, bf16[4096,2048]{1,0:T(8,128)(2,1)} %w_hbm.1, ...), custom_call_target="tpu_custom_call" | custom-call | tf_op jit(solution)/shard_map/hybrid/pallas_call | solution.py:606
  197.5 2.3 %copy.27 = bf16[256,2048]{1,0:T(8,128)(2,1)} copy(bf16[256,2048]{1,0:T(8,128)(2,1)} %get-tuple-element.4) | data formatting | bytes 2097152
  199.8 2.3 %copy.28 = bf16[256,2048]{1,0:T(8,128)(2,1)} copy(bf16[256,2048]{1,0:T(8,128)(2,1)} %get-tuple-element.5) | data formatting | bytes 2097152
where the time goes:
time: 203 us; the launch traced here: 202 us
  Pallas kernels  187 us (92%)
  local copies, waits for them, and re-layouts  14.6 us (7%)
    pallas_call x1, Pallas kernels, per_device(): pl.pallas_call(kernel, out_shape=(jax.ShapeDtypeStruct((ROWS, WIDE), BF16...  187 us
    unnamed x7, local copies, waits for them, and re-layouts  11.3 us

commit v1 on v0

--- a/solution.py
+++ b/solution.py
@@ -20,6 +20,7 @@
 PAIRS = 16
 NSTATE = 256
 MSG = 80
+GROUP = 8 * ROWS
 COEF = 1.4426950408889634 / (HD**0.5)
 NT = (((1,), (1,)), ((), ()))
 TN = (((0,), (0,)), ((), ()))
@@ -92,7 +93,6 @@
     back,
     incoming,
     squares,
-    bar_unused,
     w_sem,
     prior_sem,
     y_send,
@@ -203,24 +203,23 @@
             for way in range(2):
                 fn(half, way)
 
-    def stage_a(p):
+    def row_sends(p, r):
+        each(lambda half, way: send_desc("p2a", p, r, half, way).start())
+
+    def own_sends(p):
         each(lambda half, way: send_desc("p1a", p, 0, half, way).start())
-        each(lambda half, way: send_desc("p2a", p, 0, half, way).start())
-
-    def stage_b(p):
+
+    def own_forwards(p):
         def got_one(half, way):
             wait_whole(neighbour(base(p), first(half), 2 * way - 1), half)
             send_desc("p1b", p, 0, half, way).start()
 
         each(got_one)
-        for r in (1, 3):
-            each(lambda half, way: send_desc("p2a", p, r, half, way).start())
-
-    def stage_c(p):
+
+    def far_row(p):
         for half in range(2):
             wait_split(neighbour(base(p), first(half), 2), half)
-        each(lambda half, way: send_desc("p2a", p, 2, half, way).start())
-        forward(p, 0)
+        row_sends(p, 2)
 
     def forward(p, r):
         def got_one(half, way):
@@ -230,12 +229,12 @@
 
         each(got_one)
 
-    def stage_d(p):
-        forward(p, 1)
-        forward(p, 3)
-
-    def stage_e(p):
-        forward(p, 2)
+    def forwards(p):
+        def one(r, carry):
+            forward(p, r)
+            return carry
+
+        lax.fori_loop(0, 4, one, 0)
 
     def stage_f(p):
         def one(r, carry):
@@ -257,16 +256,17 @@
     for copy in edge_copies:
         copy.start()
     y_copy.start()
-    stage_a(0)
+    own_sends(0)
+    row_sends(0, 0)
 
     row_i = lax.broadcasted_iota(jnp.int32, (ROWS, ROWS), 0)
     col_i = lax.broadcasted_iota(jnp.int32, (ROWS, ROWS), 1)
     lower = row_i >= col_i
     ones_low = jnp.where(lower, 1.0, 0.0).astype(F32)
     ld = ld_ref[...]
-    cum = exact_dot(ones_low, ld, (((1,), (0,)), ((), ())))
-    cum_t[...] = exact_dot(ld, ones_low, (((0,), (1,)), ((), ())))
-    dt = dt_ref[...]
+    cum = exact_dot(ones_low, ld, NT)
+    cum_t[...] = exact_dot(ld, ones_low, NT)
+    dt = exact_dot(jnp.where(row_i == col_i, 1.0, 0.0).astype(F32), dt_ref[...], NT)
     aux[:, 0:32] = cum
     aux[:, 32:64] = dt
     aux[:, 64:96] = jnp.exp(cum[ROWS - 1 : ROWS] - cum) * dt
@@ -278,15 +278,17 @@
     at_start = c == 0
 
     def conv(buffer, edge, own_prior, here, taps):
-        before = jnp.where(at_start, own_prior.astype(F32), edge.astype(F32)[8:16])
-        buffer[0:8, :] = before
+        buffer[5:8, :] = jnp.where(at_start, own_prior, edge.astype(F32)[13:16])
         buffer[8 : 8 + ROWS, :] = here.astype(F32)
         total = taps[0:1] * buffer[5 : 5 + ROWS, :]
         for k in range(1, 4):
             total = total + taps[k : k + 1] * buffer[5 + k : 5 + k + ROWS, :]
         return silu(total)
 
-    proj = conv(ext_bc, edge_bc[...], prior_bc[...], bc_ref[...], taps_bc[...])
+    flat_prior = prior_bc[...].astype(F32)
+    flat_prior = jnp.concatenate([flat_prior[:, 0], flat_prior[:, 1]], axis=1)
+    flat_taps = jnp.concatenate([taps_bc[:, 0], taps_bc[:, 1]], axis=1)
+    proj = conv(ext_bc, edge_bc[...], flat_prior, bc_ref[...], flat_taps)
     b_ref[...] = proj[:, :NSTATE].astype(BF16)
     c_ref[...] = proj[:, NSTATE:].astype(BF16)
     g_ref[...] = dot(c_ref[...], b_ref[...], NT)
@@ -307,7 +309,9 @@
 
     def local_states(pair, carry):
         cols = columns(pair)
-        act = conv(ext, edge_x[:, cols], prior_x[:, cols], x_ref[:, cols], taps_x[:, cols])
+        act = conv(
+            ext, edge_x[:, cols], prior_x[:, cols].astype(F32), x_ref[:, cols], taps_x[:, cols]
+        )
         xa[:, cols] = act
         lanes = rolled(pair)
         weighted = (act * spread(lanes, 64)).astype(BF16)
@@ -331,104 +335,86 @@
             def _():
                 got[c] = msg[h]
 
-        @pl.when(pair == 6)
-        def _():
-            stage_b(0)
-
-        @pl.when(pair == 12)
+        @pl.when(pair == 2)
+        def _():
+            own_forwards(0)
+
+        @pl.when(pair == 5)
         def _():
             y_got.wait_recv()
-            stage_a(1)
+            own_sends(1)
+            row_sends(0, 1)
+            row_sends(0, 3)
+
+        @pl.when(pair == 10)
+        def _():
+            own_forwards(1)
+            far_row(0)
+            row_sends(1, 0)
+
+        @pl.when(pair == 15)
+        def _():
+            row_sends(1, 1)
+            row_sends(1, 3)
 
         return carry
 
     lax.fori_loop(0, PAIRS, local_states, 0)
-    stage_c(0)
-
-    def within_block(pair, carry):
-        cols = columns(pair)
-        lanes = rolled(pair)
-        act = xa[:, cols]
-        scaled = (act * spread(lanes, 32)).astype(BF16)
-        parts = []
-        for sub in range(2):
-            h = 2 * pair + sub
-            diff = lanes[:, sub : sub + 1] - cum_t[pl.ds(h, 1), :]
-            decay = jnp.exp(jnp.where(lower, diff, -1e30))
-            parts.append(dot((g_ref[...] * decay).astype(BF16), scaled))
-        xa[:, cols] = jnp.where(left_half, parts[0], parts[1]) + skip_ref[:, cols] * act
-
-        @pl.when(pair == 6)
-        def _():
-            stage_b(1)
-
-        @pl.when(pair == 12)
-        def _():
-            stage_d(0)
-
-        return carry
-
-    lax.fori_loop(0, PAIRS, within_block, 0)
-    stage_e(0)
+    far_row(1)
 
     acc[...] = jnp.zeros_like(acc)
     top[...] = jnp.full(top.shape, -1e30, F32)
 
-    def attend(h, keys, vals, allowed):
-        query = q_ref[:, pl.ds(pl.multiple_of(h * HD, HD), HD)]
-        scores = dot(query, keys, NT)
-        if allowed is not None:
-            scores = jnp.where(allowed, scores, -1e30)
-        return scores
-
-    def absorb(h, scores, vals):
-        before = top[h]
-        new = jnp.maximum(before, jnp.max(scores, axis=1, keepdims=True))
-        top[h] = new
-        shrink = jnp.exp2((before - new) * COEF)
-        weights = jnp.exp2((scores - new[:, 0:1]) * COEF).astype(BF16)
+    lane = lax.broadcasted_iota(jnp.int32, (1, GROUP), 1)
+    order = 2 * lax.rem(lax.div(lane, ROWS), 4) + lax.div(lane, 4 * ROWS)
+    place = lax.rem(c, 8)
+    offset = jnp.where(order < place, ROWS, jnp.where(order == place, 0, -ROWS))
+    edge_lane = lax.rem(lane, ROWS) - offset
+    row_one = lax.broadcasted_iota(jnp.int32, (ROWS, 1), 0)
+
+    def group(x_at, part, heads_of, masked):
+        keys = kvb[pl.ds(x_at * 8, 8), part].reshape(GROUP, HD)
+        vals = kvb[pl.ds(x_at * 8, 8), part + 1].reshape(GROUP, HD)
         wide = jnp.concatenate([vals, jnp.ones_like(vals)], axis=1)
-        acc[h] = acc[h] * jnp.concatenate([shrink, shrink], axis=1) + dot(weights, wide)
+
+        def attend(h):
+            query = q_ref[:, pl.ds(pl.multiple_of(h * HD, HD), HD)]
+            scores = dot(query, keys, NT)
+            if masked:
+                scores = jnp.where(edge_lane <= row_one, scores, -1e30)
+            return scores
+
+        def absorb(h, scores):
+            before = top[h]
+            new = jnp.maximum(before, jnp.max(scores, axis=1, keepdims=True))
+            top[h] = new
+            shrink = jnp.exp2((before - new) * COEF)
+            weights = jnp.exp2((scores - new[:, 0:1]) * COEF).astype(BF16)
+            acc[h] = acc[h] * jnp.concatenate([shrink, shrink], axis=1) + dot(weights, wide)
+
+        ahead = attend(heads_of[0])
+        for i, h in enumerate(heads_of):
+            scores = ahead
+            if i + 1 < len(heads_of):
+                ahead = attend(heads_of[i + 1])
+            absorb(h, scores)
 
     def cached(g, carry):
         @pl.when(g == 1)
         def _():
-            stage_c(1)
+            forwards(0)
+            forwards(1)
 
         @pl.when(g == 3)
         def _():
-            stage_d(1)
-            stage_e(1)
-
-        @pl.when(g == 4)
-        def _():
             stage_f(0)
-
-        @pl.when(g == 7)
-        def _():
             stage_f(1)
 
-        plane = jnp.where((g == 3) | (g >= 5), 1, 0)
-        far = jnp.where(
-            (g == 0) | (g == 3), 0, jnp.where((g == 1) | (g == 5), 1, jnp.where((g == 2) | (g == 6), 3, 2))
-        )
-        x_at = lax.rem(lax.div(c, 8) + far, 4)
-        y_at = lax.rem(lax.rem(c, 2) + plane, 2)
-        slot = x_at * 8 + y_at * 4
-        keys = kvb[pl.ds(slot, 4), 2].reshape(4 * ROWS, HD)
-        vals = kvb[pl.ds(slot, 4), 3].reshape(4 * ROWS, HD)
-
-        def two(i, carry2):
-            s0 = attend(2 * i, keys, vals, None)
-            s1 = attend(2 * i + 1, keys, vals, None)
-            absorb(2 * i, s0, vals)
-            absorb(2 * i + 1, s1, vals)
-            return carry2
-
-        lax.fori_loop(0, HEADS // 2, two, 0)
-        return carry
-
-    lax.fori_loop(0, 8, cached, 0)
+        far = jnp.where(g == 2, 3, jnp.where(g == 3, 2, g))
+        group(lax.rem(lax.div(c, 8) + far, 4), 2, list(range(HEADS)), False)
+        return carry
+
+    lax.fori_loop(0, 4, cached, 0)
 
     prior_copy.wait()
 
@@ -469,33 +455,42 @@
             (c, lax.rem(t + i, TP)),
         )
 
-    def head_block(h, carry):
-        def whole(g, carry2):
-            slot = g * 4
-            keys = kvb[pl.ds(slot, 4), 0].reshape(4 * ROWS, HD)
-            vals = kvb[pl.ds(slot, 4), 1].reshape(4 * ROWS, HD)
-            absorb(h, attend(h, keys, vals, None), vals)
+    def block_keys(part, carry):
+        heads_of = [part * 4 + i for i in range(4)]
+
+        def earlier(x_at, carry2):
+            group(x_at, 0, heads_of, False)
             return carry2
 
-        lax.fori_loop(0, 2 * lax.div(c, 8), whole, 0)
-
-        def single(j, carry2):
-            slot = slot_of(j)
-            vals = kvb[slot, 1]
-            absorb(h, attend(h, kvb[slot, 0], vals, None), vals)
-            return carry2
-
-        lax.fori_loop(lax.div(c, 8) * 8, c, single, 0)
-        vals = kvb[own, 1]
-        absorb(h, attend(h, kvb[own, 0], vals, lower), vals)
-        full = acc[h]
-        cols = pl.ds(pl.multiple_of((t * HEADS + h) * HD, HD), HD)
-        heads[:, cols] = (full[:, :HD] / full[:, HD:]).astype(BF16)
-        for i in range(1, TP):
-            head_copy(h, i).start()
-        return carry
-
-    lax.fori_loop(0, HEADS, head_block, 0)
+        lax.fori_loop(0, lax.div(c, 8), earlier, 0)
+        group(lax.div(c, 8), 0, heads_of, True)
+        for h in heads_of:
+            full = acc[h]
+            cols = pl.ds(pl.multiple_of((t * HEADS + h) * HD, HD), HD)
+            heads[:, cols] = (full[:, :HD] / full[:, HD:]).astype(BF16)
+            for i in range(1, TP):
+                head_copy(h, i).start()
+        return carry
+
+    lax.fori_loop(0, 2, block_keys, 0)
+
+    def within_block(pair, carry):
+        cols = columns(pair)
+        lanes = rolled(pair)
+        act = xa[:, cols]
+        scaled = (act * spread(lanes, 32)).astype(BF16)
+        skips = jnp.where(left_half, skip_ref[2 * pair], skip_ref[2 * pair + 1])
+        parts = []
+        for sub in range(2):
+            h = 2 * pair + sub
+            diff = lanes[:, sub : sub + 1] - cum_t[pl.ds(h, 1), :]
+            decay = jnp.exp(jnp.where(lower, diff, -1e30))
+            parts.append(dot((g_ref[...] * decay).astype(BF16), scaled))
+        xa[:, cols] = jnp.where(left_half, parts[0], parts[1]) + skips * act
+
+        return carry
+
+    lax.fori_loop(0, PAIRS, within_block, 0)
 
     def in_wait(j, carry):
         @pl.when(j != c)
@@ -602,14 +597,14 @@
 ):
     vm = pl.BlockSpec(memory_space=pltpu.VMEM)
     anywhere = pl.BlockSpec(memory_space=pl.ANY)
-    pad = ((5, 0), (0, 0))
+    small = pl.BlockSpec(memory_space=pltpu.SMEM)
     return pl.pallas_call(
         kernel,
         out_shape=(
             jax.ShapeDtypeStruct((ROWS, WIDE), BF16),
             jax.ShapeDtypeStruct((ROWS, WIDE), BF16),
         ),
-        in_specs=[vm] * 5 + [anywhere] + [vm] * 10 + [anywhere, vm],
+        in_specs=[vm] * 5 + [anywhere] + [vm] * 9 + [small, anywhere, vm],
         out_specs=(vm, vm),
         scratch_shapes=[
             pltpu.VMEM((CTX, 4, ROWS, HD), BF16),
@@ -633,7 +628,6 @@
             pltpu.VMEM((CTX, 64, NSTATE), BF16),
             pltpu.VMEM((WIDE, NSTATE), BF16),
             pltpu.VMEM((ROWS, 128), F32),
-            pltpu.VMEM((8, 128), F32),
             pltpu.SemaphoreType.DMA,
             pltpu.SemaphoreType.DMA,
             pltpu.SemaphoreType.DMA,
@@ -664,12 +658,12 @@
         ssm_bc.reshape(ROWS, 2 * NSTATE),
         gate_z,
         conv_x,
-        conv_bc.reshape(4, 2 * NSTATE),
-        jnp.pad(conv_prior_x, pad),
-        jnp.pad(conv_prior_bc.reshape(3, 2 * NSTATE), pad),
-        step_dt,
-        log_decay,
-        jnp.repeat(skip_d, 64).reshape(1, WIDE),
+        conv_bc,
+        conv_prior_x,
+        conv_prior_bc,
+        step_dt.T,
+        log_decay.T,
+        skip_d,
         ssm_prior.reshape(WIDE, NSTATE),
         norm_gain.reshape(1, WIDE),
     )

time: 203 us -> 145 us (0.71)
  the two profiles are of different devices: /device:TPU:118 before, /device:TPU:6 now
where the time goes in v1:
time: 145 us; the launch traced here: 144 us
  Pallas kernels  137 us (94%)
  local copies, waits for them, and re-layouts  6.29 us (4%)
    pallas_call x1, Pallas kernels, per_device(): pl.pallas_call(kernel, out_shape=(jax.ShapeDtypeStruct((ROWS, WIDE), BF16...  137 us
    unnamed x3, local copies, waits for them, and re-layouts  6.29 us

profile of v1, /device:TPU:6, one launch (start us, length us, event | category | flops | bytes accessed | tf_op | source)
XLA Modules:
  0.0 144.3 jit_solution(6512580465081883593)
XLA Ops:
  0.6 1.7 %copy.20 = bf16[32,8,2,256]{3,1,2,0:T(8,128)(2,1)} copy(bf16[32,8,2,256]{3,2,1,0:T(2,128)(2,1)} %bitcast.8) | data formatting | bytes 524288
  2.3 137.4 %hybrid.1 = (bf16[256,2048]{1,0:T(8,128)(2,1)}, bf16[256,2048]{1,0:T(8,128)(2,1)}) custom-call(bf16[256,1024]{1,0:T(8,128)(2,1)} %q_ref.1, bf16[256,128]{1,0:T(8,128)(2,1)} %k_ref.1, bf16[256,128]{1,0:T(8,128)(2,1)} %v_ref.1, bf16[256,128]{1,0:T(8,128)(2,1)} %pk_ref.1, bf16[256,128]{1,0:T(8,128)(2,1)} %pv_ref.1, bf16[4096,2048]{1,0:T(8,128)(2,1)} %w_hbm.1, ...), custom_call_target="tpu_custom_call" | custom-call | tf_op jit(solution)/shard_map/hybrid/pallas_call | solution.py:601
  139.7 2.3 %copy.23 = bf16[256,2048]{1,0:T(8,128)(2,1)} copy(bf16[256,2048]{1,0:T(8,128)(2,1)} %get-tuple-element.4) | data formatting | bytes 2097152
  142.0 2.3 %copy.24 = bf16[256,2048]{1,0:T(8,128)(2,1)} copy(bf16[256,2048]{1,0:T(8,128)(2,1)} %get-tuple-element.5) | data formatting | bytes 2097152

commit v2 on v1

--- a/solution.py
+++ b/solution.py
@@ -47,8 +47,9 @@
     return c + 2 * (lax.rem(z + step + 4, 4) - z)
 
 
-def slot_of(c):
-    return lax.div(c, 8) * 8 + lax.rem(c, 2) * 4 + lax.rem(lax.div(c, 2), 4)
+def slot_of(c, half):
+    x, z, y = lax.div(c, 8), lax.rem(lax.div(c, 2), 4), lax.rem(c, 2)
+    return z * 8 + y * 4 + x if half == 0 else x * 8 + y * 4 + z
 
 
 def kernel(
@@ -128,12 +129,6 @@
         prior_hbm.at[pl.ds(pl.multiple_of(c * 64, 64), 64)], state, prior_sem
     )
     prior_copy.start()
-    own = slot_of(c)
-    kvb[own, 0] = k_ref[...]
-    kvb[own, 1] = v_ref[...]
-    kvb[own, 2] = pk_ref[...]
-    kvb[own, 3] = pv_ref[...]
-
     barrier = pltpu.get_barrier_semaphore()
 
     def greet_ctx(i, carry):
@@ -150,6 +145,24 @@
 
     lax.fori_loop(1, CTX, greet_ctx, 0)
     lax.fori_loop(1, TP, greet_tp, 0)
+    kvb[0, slot_of(c, 0), 0] = k_ref[...]
+    kvb[0, slot_of(c, 0), 1] = v_ref[...]
+    kvb[1, slot_of(c, 1), 0] = pk_ref[...]
+    kvb[1, slot_of(c, 1), 1] = pv_ref[...]
+
+    row_i = lax.broadcasted_iota(jnp.int32, (ROWS, ROWS), 0)
+    col_i = lax.broadcasted_iota(jnp.int32, (ROWS, ROWS), 1)
+    lower = row_i >= col_i
+    ones_low = jnp.where(lower, 1.0, 0.0).astype(F32)
+    ld = ld_ref[...]
+    cum = exact_dot(ones_low, ld, NT)
+    cum_t[...] = exact_dot(ld, ones_low, NT)
+    dt = exact_dot(jnp.where(row_i == col_i, 1.0, 0.0).astype(F32), dt_ref[...], NT)
+    aux[:, 0:32] = cum
+    aux[:, 32:64] = dt
+    aux[:, 64:96] = jnp.exp(cum[ROWS - 1 : ROWS] - cum) * dt
+    aux[:, 96:128] = jnp.exp(cum)
+
     pl.semaphore_wait(barrier, CTX - 1 + TP - 1)
 
     def first(half):
@@ -157,11 +170,11 @@
 
     def piece(slot, half, quarter):
         if quarter is None:
-            return kvb.at[slot, pl.ds(2 * half, 2)]
-        return kvb.at[slot, 2 * half + quarter]
+            return kvb.at[half, slot]
+        return kvb.at[half, slot, quarter]
 
     def kv_copy(chunk, half, quarter, send, dest):
-        slot = slot_of(chunk)
+        slot = slot_of(chunk, half)
         ref = piece(slot, half, quarter)
         recv = kv_recv.at[slot, half, 0 if quarter is None else quarter]
         return remote(ref, ref, send, recv, (dest, t))
@@ -245,8 +258,9 @@
 
         lax.fori_loop(0, 4, one, 0)
 
-    y_copy = remote(kvb.at[own], kvb.at[own], y_send, y_recv, (mate, t))
-    y_got = remote(kvb.at[slot_of(mate)], kvb.at[slot_of(mate)], y_send, y_recv, (mate, t))
+    def y_copy(half, owner):
+        ref = kvb.at[half, slot_of(owner, half)]
+        return remote(ref, ref, y_send.at[half], y_recv.at[half], (mate, t))
 
     following = lax.rem(c + 1, CTX)
     edge_copies = [
@@ -255,22 +269,10 @@
     ]
     for copy in edge_copies:
         copy.start()
-    y_copy.start()
+    for half in range(2):
+        y_copy(half, c).start()
     own_sends(0)
     row_sends(0, 0)
-
-    row_i = lax.broadcasted_iota(jnp.int32, (ROWS, ROWS), 0)
-    col_i = lax.broadcasted_iota(jnp.int32, (ROWS, ROWS), 1)
-    lower = row_i >= col_i
-    ones_low = jnp.where(lower, 1.0, 0.0).astype(F32)
-    ld = ld_ref[...]
-    cum = exact_dot(ones_low, ld, NT)
-    cum_t[...] = exact_dot(ld, ones_low, NT)
-    dt = exact_dot(jnp.where(row_i == col_i, 1.0, 0.0).astype(F32), dt_ref[...], NT)
-    aux[:, 0:32] = cum
-    aux[:, 32:64] = dt
-    aux[:, 64:96] = jnp.exp(cum[ROWS - 1 : ROWS] - cum) * dt
-    aux[:, 96:128] = jnp.exp(cum)
 
     for copy in edge_copies:
         copy.wait_recv()
@@ -341,7 +343,8 @@
 
         @pl.when(pair == 5)
         def _():
-            y_got.wait_recv()
+            for half in range(2):
+                y_copy(half, mate).wait_recv()
             own_sends(1)
             row_sends(0, 1)
             row_sends(0, 3)
@@ -366,21 +369,21 @@
     top[...] = jnp.full(top.shape, -1e30, F32)
 
     lane = lax.broadcasted_iota(jnp.int32, (1, GROUP), 1)
-    order = 2 * lax.rem(lax.div(lane, ROWS), 4) + lax.div(lane, 4 * ROWS)
-    place = lax.rem(c, 8)
-    offset = jnp.where(order < place, ROWS, jnp.where(order == place, 0, -ROWS))
-    edge_lane = lax.rem(lane, ROWS) - offset
     row_one = lax.broadcasted_iota(jnp.int32, (ROWS, 1), 0)
 
-    def group(x_at, part, heads_of, masked):
-        keys = kvb[pl.ds(x_at * 8, 8), part].reshape(GROUP, HD)
-        vals = kvb[pl.ds(x_at * 8, 8), part + 1].reshape(GROUP, HD)
+    def group(half, at, heads_of):
+        keys = kvb[half, pl.ds(at * 8, 8), 0].reshape(GROUP, HD)
+        vals = kvb[half, pl.ds(at * 8, 8), 1].reshape(GROUP, HD)
         wide = jnp.concatenate([vals, jnp.ones_like(vals)], axis=1)
+        if half == 0:
+            order = lax.rem(lax.div(lane, ROWS), 4) * 8 + at * 2 + lax.div(lane, 4 * ROWS)
+            offset = jnp.where(order < c, ROWS, jnp.where(order == c, 0, -ROWS))
+            edge_lane = lax.rem(lane, ROWS) - offset
 
         def attend(h):
             query = q_ref[:, pl.ds(pl.multiple_of(h * HD, HD), HD)]
             scores = dot(query, keys, NT)
-            if masked:
+            if half == 0:
                 scores = jnp.where(edge_lane <= row_one, scores, -1e30)
             return scores
 
@@ -399,23 +402,6 @@
                 ahead = attend(heads_of[i + 1])
             absorb(h, scores)
 
-    def cached(g, carry):
-        @pl.when(g == 1)
-        def _():
-            forwards(0)
-            forwards(1)
-
-        @pl.when(g == 3)
-        def _():
-            stage_f(0)
-            stage_f(1)
-
-        far = jnp.where(g == 2, 3, jnp.where(g == 3, 2, g))
-        group(lax.rem(lax.div(c, 8) + far, 4), 2, list(range(HEADS)), False)
-        return carry
-
-    lax.fori_loop(0, 4, cached, 0)
-
     prior_copy.wait()
 
     def back_copy(j):
@@ -443,36 +429,6 @@
         state[...] = jnp.exp(total) * now + got[j, 0:64, :].astype(F32)
         return carry
 
-    lax.fori_loop(0, CTX, scan, 0)
-
-    def head_copy(h, i):
-        cols = pl.ds(pl.multiple_of((t * HEADS + h) * HD, HD), HD)
-        return remote(
-            heads.at[:, cols],
-            heads.at[:, cols],
-            hd_send.at[h, i],
-            hd_recv.at[t, h],
-            (c, lax.rem(t + i, TP)),
-        )
-
-    def block_keys(part, carry):
-        heads_of = [part * 4 + i for i in range(4)]
-
-        def earlier(x_at, carry2):
-            group(x_at, 0, heads_of, False)
-            return carry2
-
-        lax.fori_loop(0, lax.div(c, 8), earlier, 0)
-        group(lax.div(c, 8), 0, heads_of, True)
-        for h in heads_of:
-            full = acc[h]
-            cols = pl.ds(pl.multiple_of((t * HEADS + h) * HD, HD), HD)
-            heads[:, cols] = (full[:, :HD] / full[:, HD:]).astype(BF16)
-            for i in range(1, TP):
-                head_copy(h, i).start()
-        return carry
-
-    lax.fori_loop(0, 2, block_keys, 0)
 
     def within_block(pair, carry):
         cols = columns(pair)
@@ -490,7 +446,61 @@
 
         return carry
 
-    lax.fori_loop(0, PAIRS, within_block, 0)
+
+    def at_of(half, far):
+        here = lax.div(c, 8) if half == 1 else lax.rem(lax.div(c, 2), 4)
+        return lax.rem(here + far, 4)
+
+    def near(g, carry):
+        far = jnp.where(g == 2, 3, g)
+
+        @pl.when(g == 1)
+        def _():
+            lax.fori_loop(0, PAIRS, within_block, 0)
+            forwards(1)
+
+        group(1, at_of(1, far), list(range(HEADS)))
+
+        @pl.when(g == 0)
+        def _():
+            forwards(0)
+
+        group(0, at_of(0, far), list(range(HEADS)))
+        return carry
+
+    lax.fori_loop(0, 3, near, 0)
+    stage_f(0)
+    stage_f(1)
+    lax.fori_loop(0, CTX, scan, 0)
+
+    other_core = t + 1 - 2 * lax.rem(t, 2)
+    across = lax.rem(t + 2, TP)
+
+    def head_copy(src, h, dest, kind):
+        cols = pl.ds(pl.multiple_of((src * HEADS + h) * HD, HD), HD)
+        return remote(
+            heads.at[:, cols], heads.at[:, cols], hd_send.at[h, kind], hd_recv.at[src, h], (c, dest)
+        )
+
+    def pass_on(h, carry):
+        head_copy(across, h, across, 0).wait_recv()
+        head_copy(across, h, other_core, 2).start()
+        return carry
+
+    def last(part, carry):
+        heads_of = [part * 4 + i for i in range(4)]
+        group(1, at_of(1, 2), heads_of)
+        group(0, at_of(0, 2), heads_of)
+        for h in heads_of:
+            full = acc[h]
+            cols = pl.ds(pl.multiple_of((t * HEADS + h) * HD, HD), HD)
+            heads[:, cols] = (full[:, :HD] / full[:, HD:]).astype(BF16)
+            head_copy(t, h, across, 0).start()
+            head_copy(t, h, other_core, 1).start()
+        return carry
+
+    lax.fori_loop(0, 2, last, 0)
+    lax.fori_loop(0, 4, pass_on, 0)
 
     def in_wait(j, carry):
         @pl.when(j != c)
@@ -524,13 +534,11 @@
 
     lax.fori_loop(0, PAIRS, norm, 0)
 
+    lax.fori_loop(4, HEADS, pass_on, 0)
+
     def head_wait(h, carry):
-        for i in range(1, TP):
-            src = lax.rem(t + i, TP)
-            cols = pl.ds(pl.multiple_of((src * HEADS + h) * HD, HD), HD)
-            remote(
-                heads.at[:, cols], heads.at[:, cols], hd_send.at[h, i], hd_recv.at[src, h], (c, src)
-            ).wait_recv()
+        head_copy(other_core, h, other_core, 1).wait_recv()
+        head_copy(lax.rem(other_core + 2, TP), h, other_core, 2).wait_recv()
         return carry
 
     lax.fori_loop(0, HEADS, head_wait, 0)
@@ -545,7 +553,8 @@
 
     for copy in edge_copies:
         copy.wait_send()
-    y_copy.wait_send()
+    for half in range(2):
+        y_copy(half, c).wait_send()
     for p in range(2):
         each(lambda half, way: send_desc("p1a", p, 0, half, way).wait_send())
         each(lambda half, way: send_desc("p1b", p, 0, half, way).wait_send())
@@ -568,8 +577,9 @@
     lax.fori_loop(0, CTX, states_sent, 0)
 
     def heads_sent(h, carry):
-        for i in range(1, TP):
-            head_copy(h, i).wait_send()
+        head_copy(t, h, across, 0).wait_send()
+        head_copy(t, h, other_core, 1).wait_send()
+        head_copy(across, h, other_core, 2).wait_send()
         return carry
 
     lax.fori_loop(0, HEADS, heads_sent, 0)
@@ -607,7 +617,7 @@
         in_specs=[vm] * 5 + [anywhere] + [vm] * 9 + [small, anywhere, vm],
         out_specs=(vm, vm),
         scratch_shapes=[
-            pltpu.VMEM((CTX, 4, ROWS, HD), BF16),
+            pltpu.VMEM((2, CTX, 2, ROWS, HD), BF16),
             pltpu.VMEM((HEADS, ROWS, 2 * HD), F32),
             pltpu.VMEM((HEADS, ROWS, HD), F32),
             pltpu.VMEM((ROWS, TP * HEADS * HD), BF16),
@@ -630,8 +640,8 @@
             pltpu.VMEM((ROWS, 128), F32),
             pltpu.SemaphoreType.DMA,
             pltpu.SemaphoreType.DMA,
-            pltpu.SemaphoreType.DMA,
-            pltpu.SemaphoreType.DMA,
+            pltpu.SemaphoreType.DMA((2,)),
+            pltpu.SemaphoreType.DMA((2,)),
             pltpu.SemaphoreType.DMA((2, 10, 2, 2)),
             pltpu.SemaphoreType.DMA((CTX, 2, 2)),
             pltpu.SemaphoreType.DMA((2,)),
@@ -640,7 +650,7 @@
             pltpu.SemaphoreType.DMA((CTX,)),
             pltpu.SemaphoreType.DMA((CTX,)),
             pltpu.SemaphoreType.DMA((CTX,)),
-            pltpu.SemaphoreType.DMA((HEADS, TP)),
+            pltpu.SemaphoreType.DMA((HEADS, 3)),
             pltpu.SemaphoreType.DMA((TP, HEADS)),
         ],
         compiler_params=pltpu.CompilerParams(

time: 145 us -> 136 us (0.938)
  the two profiles are of different devices: /device:TPU:6 before, /device:TPU:3 now
where the time goes in v2:
time: 136 us
  Pallas kernels  129 us (95%)
  local copies, waits for them, and re-layouts  6.29 us (5%)
    pallas_call x1, Pallas kernels, per_device(): pl.pallas_call(kernel, out_shape=(jax.ShapeDtypeStruct((ROWS, WIDE), BF16...  129 us
    unnamed x3, local copies, waits for them, and re-layouts  6.29 us

profile of v2, /device:TPU:3, one launch (start us, length us, event | category | flops | bytes accessed | tf_op | source)
XLA Modules:
  0.0 136.2 jit_solution(6496638242078720198)
XLA Ops:
  0.6 1.7 %copy.20 = bf16[32,8,2,256]{3,1,2,0:T(8,128)(2,1)} copy(bf16[32,8,2,256]{3,2,1,0:T(2,128)(2,1)} %bitcast.8) | data formatting | bytes 524288
  2.3 129.2 %hybrid.1 = (bf16[256,2048]{1,0:T(8,128)(2,1)}, bf16[256,2048]{1,0:T(8,128)(2,1)}) custom-call(bf16[256,1024]{1,0:T(8,128)(2,1)} %q_ref.1, bf16[256,128]{1,0:T(8,128)(2,1)} %k_ref.1, bf16[256,128]{1,0:T(8,128)(2,1)} %v_ref.1, bf16[256,128]{1,0:T(8,128)(2,1)} %pk_ref.1, bf16[256,128]{1,0:T(8,128)(2,1)} %pv_ref.1, bf16[4096,2048]{1,0:T(8,128)(2,1)} %w_hbm.1, ...), custom_call_target="tpu_custom_call" | custom-call | tf_op jit(solution)/shard_map/hybrid/pallas_call | solution.py:611
  131.6 2.3 %copy.23 = bf16[256,2048]{1,0:T(8,128)(2,1)} copy(bf16[256,2048]{1,0:T(8,128)(2,1)} %get-tuple-element.4) | data formatting | bytes 2097152
  133.9 2.3 %copy.24 = bf16[256,2048]{1,0:T(8,128)(2,1)} copy(bf16[256,2048]{1,0:T(8,128)(2,1)} %get-tuple-element.5) | data formatting | bytes 2097152

commit v3 on v2

--- a/solution.py
+++ b/solution.py
@@ -21,6 +21,7 @@
 NSTATE = 256
 MSG = 80
 GROUP = 8 * ROWS
+SPOTS = CTX // 2
 COEF = 1.4426950408889634 / (HD**0.5)
 NT = (((1,), (1,)), ((), ()))
 TN = (((0,), (0,)), ((), ()))
@@ -89,9 +90,13 @@
     cum_t,
     xa,
     msg,
+    from_mate,
+    comb,
     got,
     state,
     back,
+    inc_pair,
+    out_mate,
     incoming,
     squares,
     w_sem,
@@ -102,16 +107,24 @@
     kv_recv,
     edge_send,
     edge_recv,
+    mate_send,
+    mate_recv,
     st_send,
     st_recv,
     in_send,
     in_recv,
+    out_send,
+    out_recv,
     hd_send,
     hd_recv,
 ):
     c = lax.axis_index("ctx")
     t = lax.axis_index("tp")
-    mate = c + 1 - 2 * lax.rem(c, 2)
+    side = lax.rem(c, 2)
+    spot = lax.div(c, 2)
+    mate = c + 1 - 2 * side
+    mine = SPOTS * side
+    theirs = SPOTS * (1 - side)
 
     def remote(src, dst, send, recv, dev):
         return pltpu.make_async_remote_copy(
@@ -126,25 +139,23 @@
     w_copy = pltpu.make_async_copy(w_hbm, w_ref, w_sem)
     w_copy.start()
     prior_copy = pltpu.make_async_copy(
-        prior_hbm.at[pl.ds(pl.multiple_of(c * 64, 64), 64)], state, prior_sem
+        prior_hbm.at[pl.ds(pl.multiple_of((mine + spot) * 64, 64), 64)], state, prior_sem
     )
     prior_copy.start()
     barrier = pltpu.get_barrier_semaphore()
 
+    def greet(dev):
+        pl.semaphore_signal(barrier, inc=1, device_id=dev, device_id_type=MESH)
+
     def greet_ctx(i, carry):
-        pl.semaphore_signal(
-            barrier, inc=1, device_id=(lax.rem(c + i, CTX), t), device_id_type=MESH
-        )
-        return carry
-
-    def greet_tp(i, carry):
-        pl.semaphore_signal(
-            barrier, inc=1, device_id=(c, lax.rem(t + i, TP)), device_id_type=MESH
-        )
-        return carry
-
-    lax.fori_loop(1, CTX, greet_ctx, 0)
-    lax.fori_loop(1, TP, greet_tp, 0)
+        greet((2 * lax.rem(spot + i, SPOTS) + side, t))
+        return carry
+
+    lax.fori_loop(1, SPOTS, greet_ctx, 0)
+    greet((mate, t))
+    greet((lax.rem(c + 2 * side - 1 + CTX, CTX), t))
+    greet((c, t + 1 - 2 * lax.rem(t, 2)))
+    greet((c, lax.rem(t + 2, TP)))
     kvb[0, slot_of(c, 0), 0] = k_ref[...]
     kvb[0, slot_of(c, 0), 1] = v_ref[...]
     kvb[1, slot_of(c, 1), 0] = pk_ref[...]
@@ -163,7 +174,7 @@
     aux[:, 64:96] = jnp.exp(cum[ROWS - 1 : ROWS] - cum) * dt
     aux[:, 96:128] = jnp.exp(cum)
 
-    pl.semaphore_wait(barrier, CTX - 1 + TP - 1)
+    pl.semaphore_wait(barrier, SPOTS + 3)
 
     def first(half):
         return 0 if half == 0 else 1
@@ -306,10 +317,29 @@
     def spread(lanes, at):
         return jnp.where(left_half, lanes[:, at : at + 1], lanes[:, at + 1 : at + 2])
 
-    def state_copy(h):
-        return remote(msg.at[h], got.at[c], st_send.at[h], st_recv.at[c], (h, t))
-
-    def local_states(pair, carry):
+    def mate_copy(q):
+        return remote(
+            msg.at[pl.ds(theirs + 4 * q, 4)],
+            from_mate.at[pl.ds(4 * q, 4)],
+            mate_send.at[q],
+            mate_recv.at[q],
+            (mate, t),
+        )
+
+    def decay_rows(total):
+        row = lax.broadcasted_iota(jnp.int32, (16, NSTATE), 0)
+        hi = total.astype(BF16).astype(F32)
+        mid = (total - hi).astype(BF16).astype(F32)
+        low = total - hi - mid
+        parts = jnp.where(row == 0, hi, jnp.where(row == 1, mid, jnp.where(row == 2, low, 0.0)))
+        return parts.astype(BF16)
+
+    def decay_of(rows):
+        tail = rows.astype(F32)
+        return tail[0:1] + tail[1:2] + tail[2:3]
+
+    def local_states(step, carry):
+        pair = lax.rem(step + lax.div(theirs, 2), PAIRS)
         cols = columns(pair)
         act = conv(
             ext, edge_x[:, cols], prior_x[:, cols].astype(F32), x_ref[:, cols], taps_x[:, cols]
@@ -318,30 +348,21 @@
         lanes = rolled(pair)
         weighted = (act * spread(lanes, 64)).astype(BF16)
         made = dot(weighted, b_ref[...], TN).astype(BF16)
-        row = lax.broadcasted_iota(jnp.int32, (16, NSTATE), 0)
         for sub in range(2):
             h = 2 * pair + sub
             msg[h, 0:64, :] = made[64 * sub : 64 * sub + 64]
             total = jnp.broadcast_to(lanes[ROWS - 1 : ROWS, sub : sub + 1], (16, NSTATE))
-            hi = total.astype(BF16).astype(F32)
-            mid = (total - hi).astype(BF16).astype(F32)
-            low = total - hi - mid
-            parts = jnp.where(row == 0, hi, jnp.where(row == 1, mid, jnp.where(row == 2, low, 0.0)))
-            msg[h, 64:80, :] = parts.astype(BF16)
-
-            @pl.when(h != c)
-            def _():
-                state_copy(h).start()
-
-            @pl.when(h == c)
-            def _():
-                got[c] = msg[h]
-
-        @pl.when(pair == 2)
+            msg[h, 64:80, :] = decay_rows(total)
+
+        @pl.when((step < 8) & (lax.rem(step, 2) == 1))
+        def _():
+            mate_copy(lax.div(step, 2)).start()
+
+        @pl.when(step == 2)
         def _():
             own_forwards(0)
 
-        @pl.when(pair == 5)
+        @pl.when(step == 5)
         def _():
             for half in range(2):
                 y_copy(half, mate).wait_recv()
@@ -349,13 +370,13 @@
             row_sends(0, 1)
             row_sends(0, 3)
 
-        @pl.when(pair == 10)
+        @pl.when(step == 10)
         def _():
             own_forwards(1)
             far_row(0)
             row_sends(1, 0)
 
-        @pl.when(pair == 15)
+        @pl.when(step == 15)
         def _():
             row_sends(1, 1)
             row_sends(1, 3)
@@ -404,31 +425,87 @@
 
     prior_copy.wait()
 
-    def back_copy(j):
-        here = pl.ds(pl.multiple_of(c * 64, 64), 64)
-        return remote(back.at[j], incoming.at[here], in_send.at[j], in_recv.at[c], (j, t))
+    def pair_copy(i, source):
+        return remote(
+            comb.at[i], got.at[source], st_send.at[i], st_recv.at[source], (2 * i + side, t)
+        )
+
+    def back_copy(j, owner):
+        return remote(
+            back.at[j], inc_pair.at[owner], in_send.at[j], in_recv.at[owner], (2 * j + side, t)
+        )
+
+    def out_copy(q, half_at):
+        return remote(
+            out_mate.at[pl.ds(pl.multiple_of(q * 256, 256), 256)],
+            incoming.at[pl.ds(pl.multiple_of(half_at * 64 + q * 256, 256), 256)],
+            out_send.at[q],
+            out_recv.at[q],
+            (mate, t),
+        )
+
+    def earlier_of(i):
+        own_total = decay_of(msg[mine + i, 64:80, :])
+        mate_total = decay_of(from_mate[i, 64:80, :])
+        own_state = msg[mine + i, 0:64, :].astype(F32)
+        mate_state = from_mate[i, 0:64, :].astype(F32)
+        first_side = side == 0
+        return (
+            jnp.where(first_side, own_total, mate_total),
+            jnp.where(first_side, own_state, mate_state),
+            jnp.where(first_side, mate_total, own_total),
+            jnp.where(first_side, mate_state, own_state),
+        )
+
+    def combine(step, carry):
+        i = lax.rem(spot + step, SPOTS)
+        early_total, early_state, late_total, late_state = earlier_of(i)
+        comb[i, 0:64, :] = (jnp.exp(late_total) * early_state + late_state).astype(BF16)
+        comb[i, 64:80, :] = decay_rows(jnp.broadcast_to(early_total + late_total, (16, NSTATE)))
+
+        @pl.when(step != 0)
+        def _():
+            pair_copy(i, spot).start()
+
+        @pl.when(step == 0)
+        def _():
+            got[spot] = comb[i]
+
+        return carry
 
     def scan(j, carry):
-        @pl.when(j != c)
-        def _():
-            remote(msg.at[j], got.at[j], st_send.at[j], st_recv.at[j], (j, t)).wait_recv()
+        @pl.when(j != spot)
+        def _():
+            pair_copy(j, j).wait_recv()
 
         now = state[...]
         back[j] = now.astype(BF16)
-
-        @pl.when(j != c)
-        def _():
-            back_copy(j).start()
-
-        @pl.when(j == c)
-        def _():
-            incoming[pl.ds(pl.multiple_of(c * 64, 64), 64), :] = now.astype(BF16)
-
-        tail = got[j, 64:80, :].astype(F32)
-        total = tail[0:1] + tail[1:2] + tail[2:3]
-        state[...] = jnp.exp(total) * now + got[j, 0:64, :].astype(F32)
-        return carry
-
+        state[...] = jnp.exp(decay_of(got[j, 64:80, :])) * now + got[j, 0:64, :].astype(F32)
+        return carry
+
+    def give_back(i, carry):
+        back_copy(lax.rem(spot + i, SPOTS), spot).start()
+        return carry
+
+    def settle(i, carry):
+        @pl.when(i != spot)
+        def _():
+            back_copy(i, i).wait_recv()
+
+        early_total, early_state, _, _ = earlier_of(i)
+        entering = inc_pair[i].astype(F32)
+        after = jnp.exp(early_total) * entering + early_state
+        rows = pl.ds(pl.multiple_of((mine + i) * 64, 64), 64)
+        incoming[rows, :] = jnp.where(side == 0, entering, after).astype(BF16)
+        out_mate[pl.ds(pl.multiple_of(i * 64, 64), 64), :] = jnp.where(
+            side == 0, after, entering
+        ).astype(BF16)
+
+        @pl.when(lax.rem(i, 4) == 3)
+        def _():
+            out_copy(lax.div(i, 4), mine).start()
+
+        return carry
 
     def within_block(pair, carry):
         cols = columns(pair)
@@ -464,6 +541,19 @@
         @pl.when(g == 0)
         def _():
             forwards(0)
+            for q in range(4):
+                mate_copy(q).wait_recv()
+            lax.fori_loop(0, SPOTS, combine, 0)
+
+        @pl.when(g == 1)
+        def _():
+            lax.fori_loop(0, SPOTS, scan, 0)
+            inc_pair[spot] = back[spot]
+            lax.fori_loop(1, SPOTS, give_back, 0)
+
+        @pl.when(g == 2)
+        def _():
+            lax.fori_loop(0, SPOTS, settle, 0)
 
         group(0, at_of(0, far), list(range(HEADS)))
         return carry
@@ -471,7 +561,6 @@
     lax.fori_loop(0, 3, near, 0)
     stage_f(0)
     stage_f(1)
-    lax.fori_loop(0, CTX, scan, 0)
 
     other_core = t + 1 - 2 * lax.rem(t, 2)
     across = lax.rem(t + 2, TP)
@@ -502,15 +591,8 @@
     lax.fori_loop(0, 2, last, 0)
     lax.fori_loop(0, 4, pass_on, 0)
 
-    def in_wait(j, carry):
-        @pl.when(j != c)
-        def _():
-            rows = pl.ds(pl.multiple_of(j * 64, 64), 64)
-            remote(back.at[j], incoming.at[rows], in_send.at[j], in_recv.at[j], (j, t)).wait_recv()
-
-        return carry
-
-    lax.fori_loop(0, CTX, in_wait, 0)
+    for q in range(4):
+        out_copy(q, theirs).wait_recv()
     squares[...] = jnp.zeros_like(squares)
 
     def mix(pair, carry):
@@ -566,15 +648,17 @@
 
         lax.fori_loop(0, 4, sent, 0)
 
-    def states_sent(j, carry):
-        @pl.when(j != c)
-        def _():
-            state_copy(j).wait_send()
-            back_copy(j).wait_send()
-
-        return carry
-
-    lax.fori_loop(0, CTX, states_sent, 0)
+    for q in range(4):
+        mate_copy(q).wait_send()
+        out_copy(q, mine).wait_send()
+
+    def states_sent(step, carry):
+        i = lax.rem(spot + step, SPOTS)
+        pair_copy(i, spot).wait_send()
+        back_copy(i, spot).wait_send()
+        return carry
+
+    lax.fori_loop(1, SPOTS, states_sent, 0)
 
     def heads_sent(h, carry):
         head_copy(t, h, across, 0).wait_send()
@@ -633,9 +717,13 @@
             pltpu.VMEM((SH, ROWS), F32),
             pltpu.VMEM((ROWS, WIDE), F32),
             pltpu.VMEM((SH, MSG, NSTATE), BF16),
-            pltpu.VMEM((CTX, MSG, NSTATE), BF16),
+            pltpu.VMEM((SPOTS, MSG, NSTATE), BF16),
+            pltpu.VMEM((SPOTS, MSG, NSTATE), BF16),
+            pltpu.VMEM((SPOTS, MSG, NSTATE), BF16),
             pltpu.VMEM((64, NSTATE), F32),
-            pltpu.VMEM((CTX, 64, NSTATE), BF16),
+            pltpu.VMEM((SPOTS, 64, NSTATE), BF16),
+            pltpu.VMEM((SPOTS, 64, NSTATE), BF16),
+            pltpu.VMEM((SPOTS * 64, NSTATE), BF16),
             pltpu.VMEM((WIDE, NSTATE), BF16),
             pltpu.VMEM((ROWS, 128), F32),
             pltpu.SemaphoreType.DMA,
@@ -646,10 +734,14 @@
             pltpu.SemaphoreType.DMA((CTX, 2, 2)),
             pltpu.SemaphoreType.DMA((2,)),
             pltpu.SemaphoreType.DMA((2,)),
-            pltpu.SemaphoreType.DMA((CTX,)),
-            pltpu.SemaphoreType.DMA((CTX,)),
-            pltpu.SemaphoreType.DMA((CTX,)),
-            pltpu.SemaphoreType.DMA((CTX,)),
+            pltpu.SemaphoreType.DMA((4,)),
+            pltpu.SemaphoreType.DMA((4,)),
+            pltpu.SemaphoreType.DMA((SPOTS,)),
+            pltpu.SemaphoreType.DMA((SPOTS,)),
+            pltpu.SemaphoreType.DMA((SPOTS,)),
+            pltpu.SemaphoreType.DMA((SPOTS,)),
+            pltpu.SemaphoreType.DMA((4,)),
+            pltpu.SemaphoreType.DMA((4,)),
             pltpu.SemaphoreType.DMA((HEADS, 3)),
             pltpu.SemaphoreType.DMA((TP, HEADS)),
         ],

time: 136 us -> 117 us (0.86); the launches traced: 136 us -> 115 us
  Pallas kernels: 129 us -> 108 us
    pallas_call x1, Pallas kernels: 129 us -> 108 us  [per_device(): pl.pallas_call(kernel, out_shape=(jax.ShapeDtypeStruct((ROWS, WIDE), BF16...]
where the time goes in v3:
time: 117 us; the launch traced here: 115 us
  Pallas kernels  108 us (92%)
  local copies, waits for them, and re-layouts  6.29 us (5%)
    pallas_call x1, Pallas kernels, per_device(): pl.pallas_call(kernel, out_shape=(jax.ShapeDtypeStruct((ROWS, WIDE), BF16...  108 us
    unnamed x3, local copies, waits for them, and re-layouts  6.29 us

profile of v3, /device:TPU:3, one launch (start us, length us, event | category | flops | bytes accessed | tf_op | source)
XLA Modules:
  0.0 115.1 jit_solution(8403715664610060379)
XLA Ops:
  0.6 1.7 %copy.20 = bf16[32,8,2,256]{3,1,2,0:T(8,128)(2,1)} copy(bf16[32,8,2,256]{3,2,1,0:T(2,128)(2,1)} %bitcast.8) | data formatting | bytes 524288
  2.3 108.2 %hybrid.1 = (bf16[256,2048]{1,0:T(8,128)(2,1)}, bf16[256,2048]{1,0:T(8,128)(2,1)}) custom-call(bf16[256,1024]{1,0:T(8,128)(2,1)} %q_ref.1, bf16[256,128]{1,0:T(8,128)(2,1)} %k_ref.1, bf16[256,128]{1,0:T(8,128)(2,1)} %v_ref.1, bf16[256,128]{1,0:T(8,128)(2,1)} %pk_ref.1, bf16[256,128]{1,0:T(8,128)(2,1)} %pv_ref.1, bf16[4096,2048]{1,0:T(8,128)(2,1)} %w_hbm.1, ...), custom_call_target="tpu_custom_call" | custom-call | tf_op jit(solution)/shard_map/hybrid/pallas_call | solution.py:695
  110.5 2.3 %copy.23 = bf16[256,2048]{1,0:T(8,128)(2,1)} copy(bf16[256,2048]{1,0:T(8,128)(2,1)} %get-tuple-element.4) | data formatting | bytes 2097152
  112.8 2.3 %copy.24 = bf16[256,2048]{1,0:T(8,128)(2,1)} copy(bf16[256,2048]{1,0:T(8,128)(2,1)} %get-tuple-element.5) | data formatting | bytes 2097152

commit v4 on v3

--- a/solution.py
+++ b/solution.py
@@ -338,11 +338,10 @@
         tail = rows.astype(F32)
         return tail[0:1] + tail[1:2] + tail[2:3]
 
-    def local_states(step, carry):
-        pair = lax.rem(step + lax.div(theirs, 2), PAIRS)
+    def local_pair(pair, buffer):
         cols = columns(pair)
         act = conv(
-            ext, edge_x[:, cols], prior_x[:, cols].astype(F32), x_ref[:, cols], taps_x[:, cols]
+            buffer, edge_x[:, cols], prior_x[:, cols].astype(F32), x_ref[:, cols], taps_x[:, cols]
         )
         xa[:, cols] = act
         lanes = rolled(pair)
@@ -354,37 +353,64 @@
             total = jnp.broadcast_to(lanes[ROWS - 1 : ROWS, sub : sub + 1], (16, NSTATE))
             msg[h, 64:80, :] = decay_rows(total)
 
-        @pl.when((step < 8) & (lax.rem(step, 2) == 1))
-        def _():
-            mate_copy(lax.div(step, 2)).start()
-
-        @pl.when(step == 2)
+    def local_states(step, carry):
+        pair = lax.rem(2 * step + lax.div(theirs, 2), PAIRS)
+        local_pair(pair, ext.at[0])
+        local_pair(pair + 1, ext.at[1])
+
+        @pl.when(step < 4)
+        def _():
+            mate_copy(step).start()
+
+        @pl.when(step == 1)
         def _():
             own_forwards(0)
-
-        @pl.when(step == 5)
+            row_sends(0, 1)
+            row_sends(0, 3)
+
+        @pl.when(step == 4)
         def _():
             for half in range(2):
                 y_copy(half, mate).wait_recv()
             own_sends(1)
-            row_sends(0, 1)
-            row_sends(0, 3)
-
-        @pl.when(step == 10)
+
+        return carry
+
+    lax.fori_loop(0, PAIRS // 2, local_states, 0)
+    far_row(0)
+    row_sends(1, 0)
+
+    def within_pair(pair):
+        cols = columns(pair)
+        lanes = rolled(pair)
+        act = xa[:, cols]
+        scaled = (act * spread(lanes, 32)).astype(BF16)
+        skips = jnp.where(left_half, skip_ref[2 * pair], skip_ref[2 * pair + 1])
+        parts = []
+        for sub in range(2):
+            h = 2 * pair + sub
+            diff = lanes[:, sub : sub + 1] - cum_t[pl.ds(h, 1), :]
+            decay = jnp.exp(jnp.where(lower, diff, -1e30))
+            parts.append(dot((g_ref[...] * decay).astype(BF16), scaled))
+        return jnp.where(left_half, parts[0], parts[1]) + skips * act
+
+    def within_block(i, carry):
+        results = [within_pair(2 * i), within_pair(2 * i + 1)]
+        for sub in range(2):
+            xa[:, columns(2 * i + sub)] = results[sub]
+
+        @pl.when(i == 0)
         def _():
             own_forwards(1)
-            far_row(0)
-            row_sends(1, 0)
-
-        @pl.when(step == 15)
-        def _():
             row_sends(1, 1)
             row_sends(1, 3)
 
         return carry
 
-    lax.fori_loop(0, PAIRS, local_states, 0)
+    lax.fori_loop(0, PAIRS // 2, within_block, 0)
     far_row(1)
+    forwards(0)
+
 
     acc[...] = jnp.zeros_like(acc)
     top[...] = jnp.full(top.shape, -1e30, F32)
@@ -392,23 +418,27 @@
     lane = lax.broadcasted_iota(jnp.int32, (1, GROUP), 1)
     row_one = lax.broadcasted_iota(jnp.int32, (ROWS, 1), 0)
 
-    def group(half, at, heads_of):
-        keys = kvb[half, pl.ds(at * 8, 8), 0].reshape(GROUP, HD)
-        vals = kvb[half, pl.ds(at * 8, 8), 1].reshape(GROUP, HD)
-        wide = jnp.concatenate([vals, jnp.ones_like(vals)], axis=1)
-        if half == 0:
-            order = lax.rem(lax.div(lane, ROWS), 4) * 8 + at * 2 + lax.div(lane, 4 * ROWS)
-            offset = jnp.where(order < c, ROWS, jnp.where(order == c, 0, -ROWS))
-            edge_lane = lax.rem(lane, ROWS) - offset
-
-        def attend(h):
+    def group(*runs):
+        units = []
+        for half, at, heads_of in runs:
+            keys = kvb[half, pl.ds(at * 8, 8), 0].reshape(GROUP, HD)
+            vals = kvb[half, pl.ds(at * 8, 8), 1].reshape(GROUP, HD)
+            wide = jnp.concatenate([vals, jnp.ones_like(vals)], axis=1)
+            edge_lane = None
+            if half == 0:
+                order = lax.rem(lax.div(lane, ROWS), 4) * 8 + at * 2 + lax.div(lane, 4 * ROWS)
+                offset = jnp.where(order < c, ROWS, jnp.where(order == c, 0, -ROWS))
+                edge_lane = lax.rem(lane, ROWS) - offset
+            units += [(h, keys, wide, edge_lane) for h in heads_of]
+
+        def attend(h, keys, wide, edge_lane):
             query = q_ref[:, pl.ds(pl.multiple_of(h * HD, HD), HD)]
             scores = dot(query, keys, NT)
-            if half == 0:
+            if edge_lane is not None:
                 scores = jnp.where(edge_lane <= row_one, scores, -1e30)
             return scores
 
-        def absorb(h, scores):
+        def absorb(h, wide, scores):
             before = top[h]
             new = jnp.maximum(before, jnp.max(scores, axis=1, keepdims=True))
             top[h] = new
@@ -416,12 +446,12 @@
             weights = jnp.exp2((scores - new[:, 0:1]) * COEF).astype(BF16)
             acc[h] = acc[h] * jnp.concatenate([shrink, shrink], axis=1) + dot(weights, wide)
 
-        ahead = attend(heads_of[0])
-        for i, h in enumerate(heads_of):
+        ahead = attend(*units[0])
+        for i, unit in enumerate(units):
             scores = ahead
-            if i + 1 < len(heads_of):
-                ahead = attend(heads_of[i + 1])
-            absorb(h, scores)
+            if i + 1 < len(units):
+                ahead = attend(*units[i + 1])
+            absorb(unit[0], unit[2], scores)
 
     prior_copy.wait()
 
@@ -507,23 +537,6 @@
 
         return carry
 
-    def within_block(pair, carry):
-        cols = columns(pair)
-        lanes = rolled(pair)
-        act = xa[:, cols]
-        scaled = (act * spread(lanes, 32)).astype(BF16)
-        skips = jnp.where(left_half, skip_ref[2 * pair], skip_ref[2 * pair + 1])
-        parts = []
-        for sub in range(2):
-            h = 2 * pair + sub
-            diff = lanes[:, sub : sub + 1] - cum_t[pl.ds(h, 1), :]
-            decay = jnp.exp(jnp.where(lower, diff, -1e30))
-            parts.append(dot((g_ref[...] * decay).astype(BF16), scaled))
-        xa[:, cols] = jnp.where(left_half, parts[0], parts[1]) + skips * act
-
-        return carry
-
-
     def at_of(half, far):
         here = lax.div(c, 8) if half == 1 else lax.rem(lax.div(c, 2), 4)
         return lax.rem(here + far, 4)
@@ -531,19 +544,14 @@
     def near(g, carry):
         far = jnp.where(g == 2, 3, g)
 
-        @pl.when(g == 1)
-        def _():
-            lax.fori_loop(0, PAIRS, within_block, 0)
-            forwards(1)
-
-        group(1, at_of(1, far), list(range(HEADS)))
+        group((1, at_of(1, far), list(range(HEADS))))
 
         @pl.when(g == 0)
         def _():
-            forwards(0)
             for q in range(4):
                 mate_copy(q).wait_recv()
             lax.fori_loop(0, SPOTS, combine, 0)
+            forwards(1)
 
         @pl.when(g == 1)
         def _():
@@ -555,7 +563,7 @@
         def _():
             lax.fori_loop(0, SPOTS, settle, 0)
 
-        group(0, at_of(0, far), list(range(HEADS)))
+        group((0, at_of(0, far), list(range(HEADS))))
         return carry
 
     lax.fori_loop(0, 3, near, 0)
@@ -578,8 +586,7 @@
 
     def last(part, carry):
         heads_of = [part * 4 + i for i in range(4)]
-        group(1, at_of(1, 2), heads_of)
-        group(0, at_of(0, 2), heads_of)
+        group((1, at_of(1, 2), heads_of), (0, at_of(0, 2), heads_of))
         for h in heads_of:
             full = acc[h]
             cols = pl.ds(pl.multiple_of((t * HEADS + h) * HD, HD), HD)
@@ -595,26 +602,32 @@
         out_copy(q, theirs).wait_recv()
     squares[...] = jnp.zeros_like(squares)
 
-    def mix(pair, carry):
+    def mix_pair(pair):
         cols = columns(pair)
         lanes = rolled(pair)
         earlier = dot(c_ref[...], incoming[cols, :], NT)
         mixed = xa[:, cols] + spread(lanes, 96) * earlier
-        gated = mixed * silu(z_ref[:, cols].astype(F32))
-        squares[...] += gated * gated
-        xa[:, cols] = gated
-        return carry
-
-    lax.fori_loop(0, PAIRS, mix, 0)
+        return mixed * silu(z_ref[:, cols].astype(F32))
+
+    def mix(i, carry):
+        results = [mix_pair(4 * i + sub) for sub in range(4)]
+        parts = [gated * gated for gated in results]
+        squares[...] += (parts[0] + parts[1]) + (parts[2] + parts[3])
+        for sub in range(4):
+            xa[:, columns(4 * i + sub)] = results[sub]
+        return carry
+
+    lax.fori_loop(0, PAIRS // 4, mix, 0)
     mean = jnp.sum(squares[...], axis=1, keepdims=True) * (1.0 / WIDE)
     squares[...] = jnp.broadcast_to(lax.rsqrt(mean + 1e-05), squares.shape)
 
-    def norm(pair, carry):
-        cols = columns(pair)
-        ssm_ref[:, cols] = (xa[:, cols] * squares[...] * gain_ref[:, cols]).astype(BF16)
-        return carry
-
-    lax.fori_loop(0, PAIRS, norm, 0)
+    def norm(i, carry):
+        for sub in range(4):
+            cols = columns(4 * i + sub)
+            ssm_ref[:, cols] = (xa[:, cols] * squares[...] * gain_ref[:, cols]).astype(BF16)
+        return carry
+
+    lax.fori_loop(0, PAIRS // 4, norm, 0)
 
     lax.fori_loop(4, HEADS, pass_on, 0)
 
@@ -708,7 +721,7 @@
             pltpu.VMEM((TP * HEADS * HD, WIDE), BF16),
             pltpu.VMEM((16, WIDE), BF16),
             pltpu.VMEM((16, 2 * NSTATE), BF16),
-            pltpu.VMEM((ROWS + 8, 128), F32),
+            pltpu.VMEM((2, ROWS + 8, 128), F32),
             pltpu.VMEM((ROWS + 8, 2 * NSTATE), F32),
             pltpu.VMEM((ROWS, NSTATE), BF16),
             pltpu.VMEM((ROWS, NSTATE), BF16),

time: 117 us -> 115 us (0.983)
  no operation moved by 1% of the time
where the time goes in v4:
time: 115 us; the launch traced here: 114 us
  Pallas kernels  107 us (93%)
  local copies, waits for them, and re-layouts  6.29 us (5%)
    pallas_call x1, Pallas kernels, per_device(): pl.pallas_call(kernel, out_shape=(jax.ShapeDtypeStruct((ROWS, WIDE), BF16...  107 us
    unnamed x3, local copies, waits for them, and re-layouts  6.29 us

profile of v4, /device:TPU:3, one launch (start us, length us, event | category | flops | bytes accessed | tf_op | source)
XLA Modules:
  0.0 114.3 jit_solution(4475148353370776475)
XLA Ops:
  0.6 1.7 %copy.20 = bf16[32,8,2,256]{3,1,2,0:T(8,128)(2,1)} copy(bf16[32,8,2,256]{3,2,1,0:T(2,128)(2,1)} %bitcast.8) | data formatting | bytes 524288
  2.3 107.4 %hybrid.1 = (bf16[256,2048]{1,0:T(8,128)(2,1)}, bf16[256,2048]{1,0:T(8,128)(2,1)}) custom-call(bf16[256,1024]{1,0:T(8,128)(2,1)} %q_ref.1, bf16[256,128]{1,0:T(8,128)(2,1)} %k_ref.1, bf16[256,128]{1,0:T(8,128)(2,1)} %v_ref.1, bf16[256,128]{1,0:T(8,128)(2,1)} %pk_ref.1, bf16[256,128]{1,0:T(8,128)(2,1)} %pv_ref.1, bf16[4096,2048]{1,0:T(8,128)(2,1)} %w_hbm.1, ...), custom_call_target="tpu_custom_call" | custom-call | tf_op jit(solution)/shard_map/hybrid/pallas_call | solution.py:708
  109.7 2.3 %copy.23 = bf16[256,2048]{1,0:T(8,128)(2,1)} copy(bf16[256,2048]{1,0:T(8,128)(2,1)} %get-tuple-element.4) | data formatting | bytes 2097152
  112.0 2.3 %copy.24 = bf16[256,2048]{1,0:T(8,128)(2,1)} copy(bf16[256,2048]{1,0:T(8,128)(2,1)} %get-tuple-element.5) | data formatting | bytes 2097152
